TPU v7x, 32 devices: a whole 2x2x4 slice. The times are simulated.
32 devices in a mesh: dp: 8 (over z, core), blk: 4 (over y, x).
Axes of the slice: x: 2, y: 2, z: 4, core: 2. Of those that a mesh axis runs over, the one named last changes fastest.
Arguments:
- features: bfloat16 [8192, 12800], P(('dp', 'blk')), may hold values from -6 to 6
- cotangent: bfloat16 [8192, 12800], P(('dp', 'blk')), may hold values from -6 to 6
- send_order: int32 [32, 256], P(('dp', 'blk')), may hold values from 0 to 255, each once within a row
- pair_index: int32 [96, 2], P(('dp', 'blk')), may hold values from 0 to 1, as said below
- edge_mask: int32 [96, 128, 128], P(('dp', 'blk')), may hold values 0 or 1
- distance: float32 [96, 128, 128], P(('dp', 'blk')), may hold values from 0.8 to 4.8
- radial_weight: float32 [512, 5], replicated, may hold values from -1.5 to 1.5
- mix_weight: bfloat16 [2560, 512], replicated, may hold values from -0.25 to 0.25
- out_weight: bfloat16 [2560, 512], replicated, may hold values from -0.25 to 0.25
Outputs:
- updated: bfloat16 [8192, 12800], P(('dp', 'blk'))
- mix_grad: float32 [2560, 512], P('blk')
- out_grad: float32 [2560, 512], P('blk')
Inputs may be any that keep to these rules, and one draw needn't show every extreme that they name: `pair_index`: each device's 3 pairs are distinct; both entries are local block numbers. Each row of send_order is a permutation of the device's rows.
All inputs are finite; a program needn't handle non-finite values. No bound on the sum of `edge_mask` on one device may be relied on, other than what follows from the above.
Results may differ from a plain program's by a relative error of at most 0.0059.
Values may be sent and summed in bfloat16 or wider, within the bound.
No kernel may reach another device: no remote copies, remote signals or barrier semaphores. Data moves between devices by JAX's collectives and lax.ppermute only.
A program may use at most 192 MiB of HBM per device.

v0:
```python
import functools
import math

import jax
import jax.numpy as jnp
from jax import lax
from jax.experimental import pallas as pl
from jax.experimental.pallas import tpu as pltpu
from jax.sharding import PartitionSpec as P

LMAX = 4
BLOCK = 128
CUT_RADIUS = 5.0
EDGE_SCALE = 0.25
MOST, LAST = (0, 1, 2, 3), (4,)
ORDER = MOST + LAST
VMEM_LIMIT = 48 * 1024 * 1024
PICK_LIMIT = 60 * 1024 * 1024
GRADIENT_LIMIT = 16 * 1024 * 1024
GATE_ROWS = 16
WHOLE = pl.BlockSpec(memory_space=pltpu.VMEM)
ANY = pl.BlockSpec(memory_space=pl.ANY)
SCALARS = pl.BlockSpec(memory_space=pltpu.SMEM)


def params(*semantics, limit=VMEM_LIMIT):
    return pltpu.CompilerParams(dimension_semantics=semantics, vmem_limit_bytes=limit)


def after(value, *others):
    return lax.optimization_barrier((value, *others))[0]


def span(degrees):
    return degrees[0] ** 2, (degrees[-1] + 1) ** 2


def comps_of(degrees):
    return [comp for level in degrees for comp in range(*span((level,)))]


def tree_sum(parts):
    parts = [part.astype(jnp.float32) for part in parts]
    while len(parts) > 1:
        parts = [parts[i] + parts[i + 1] for i in range(0, len(parts), 2)]
    return parts[0].astype(jnp.bfloat16)


def chosen_rows(order_ref, rows):
    local = lax.broadcasted_iota(jnp.int32, (rows, rows), 0)
    return (local == order_ref[...]).astype(jnp.float32).T.astype(jnp.bfloat16)


def pick_kernel(
    order_ref, rows_ref, out_ref, list_ref, held_ref, ready_ref, list_sem, in_sems, out_sems, *, first
):
    count, rows, width = ready_ref.shape
    order_load = pltpu.make_async_copy(order_ref, list_ref, list_sem)
    order_load.start()
    slab = rows // in_sems.shape[0]
    loads = [
        pltpu.make_async_copy(
            rows_ref.at[pl.ds(i * slab, slab), pl.ds(first * width, count * width)],
            held_ref.at[pl.ds(i * slab, slab), :],
            in_sems.at[i],
        )
        for i in range(in_sems.shape[0])
    ]
    for load in loads:
        load.start()
    order_load.wait()
    pick = chosen_rows(list_ref, rows)
    for load in loads:
        load.wait()
    stores = []
    for i in range(count):
        ready_ref[i] = jnp.dot(
            pick, held_ref[:, i * width : (i + 1) * width], preferred_element_type=jnp.float32
        ).astype(jnp.bfloat16)
        stores.append(
            pltpu.make_async_copy(
                ready_ref.at[i], out_ref.at[:, pl.ds(i * width, width)], out_sems.at[i]
            )
        )
        stores[-1].start()
    for store in stores:
        store.wait()


def pick_rows(order, features, width, degrees):
    rows = features.shape[0]
    first, last = span(degrees)
    count = last - first
    return pl.pallas_call(
        functools.partial(pick_kernel, first=first),
        in_specs=[ANY, ANY],
        out_specs=ANY,
        out_shape=jax.ShapeDtypeStruct((rows, count * width), jnp.bfloat16),
        scratch_shapes=[
            pltpu.VMEM(order.shape, jnp.int32),
            pltpu.VMEM((rows, count * width), jnp.bfloat16),
            pltpu.VMEM((count, rows, width), jnp.bfloat16),
            pltpu.SemaphoreType.DMA,
            pltpu.SemaphoreType.DMA((8,)),
            pltpu.SemaphoreType.DMA((count,)),
        ],
        compiler_params=params(limit=PICK_LIMIT),
        name="pick_rows",
    )(order, features)


def gate_kernel(pairs_ref, mask_ref, dist_ref, weight_ref, out_ref, radial_ref, *, basis_count):
    pair, step = pl.program_id(0), pl.program_id(1)

    @pl.when((pair == 0) & (step == 0))
    def _():
        out_ref[...] = jnp.zeros_like(out_ref)

    half = math.sqrt(0.5 * math.log2(math.e))
    dist = dist_ref[0]
    scaled = dist * (half * (basis_count - 1) / CUT_RADIUS)
    centers = lax.broadcasted_iota(jnp.int32, (basis_count, BLOCK), 0).astype(jnp.float32) * half
    weights = weight_ref[...]
    levels = LMAX + 1
    for row in range(GATE_ROWS):
        offset = scaled[row : row + 1, :] - centers
        phi = jnp.exp2(-(offset * offset))
        high = phi.astype(jnp.bfloat16)
        low = (phi - high.astype(jnp.float32)).astype(jnp.bfloat16)
        radial = jnp.dot(weights, high, preferred_element_type=jnp.float32)
        radial = radial + jnp.dot(weights, low, preferred_element_type=jnp.float32)
        radial = radial[0:8] + radial[8:16]
        for level in range(levels):
            radial_ref[level, row : row + 1, :] = radial[level : level + 1, :]
    envelope = (
        (0.5 * EDGE_SCALE)
        * (jnp.cos((math.pi / CUT_RADIUS) * dist) + 1.0)
        * mask_ref[0].astype(jnp.float32)
    )
    dest = pl.multiple_of(pairs_ref[pair, 0] * BLOCK + step * GATE_ROWS, GATE_ROWS)
    src = pl.multiple_of(pairs_ref[pair, 1] * BLOCK, BLOCK)
    for level in range(levels):
        out_ref[level, pl.ds(dest, GATE_ROWS), pl.ds(src, BLOCK)] = (
            radial_ref[level] * envelope
        ).astype(jnp.bfloat16)


def gate_matrices(pairs, mask, dist, radial_weight, rows):
    count = pairs.shape[0]
    levels = radial_weight.shape[1]
    transposed = radial_weight.T
    high = transposed.astype(jnp.bfloat16)
    low = (transposed - high.astype(jnp.float32)).astype(jnp.bfloat16)
    pad = ((0, 8 - levels), (0, 0))
    weights = jnp.concatenate([jnp.pad(high, pad), jnp.pad(low, pad)], axis=0)
    kernel = functools.partial(gate_kernel, basis_count=radial_weight.shape[0])
    edges = pl.BlockSpec((1, GATE_ROWS, BLOCK), lambda p, s, pairs: (p, s, 0))
    return pl.pallas_call(
        kernel,
        grid_spec=pltpu.PrefetchScalarGridSpec(
            num_scalar_prefetch=1,
            grid=(count, BLOCK // GATE_ROWS),
            in_specs=[edges, edges, pl.BlockSpec(weights.shape, lambda p, s, pairs: (0, 0))],
            out_specs=pl.BlockSpec((levels, rows, rows), lambda p, s, pairs: (0, 0, 0)),
            scratch_shapes=[pltpu.VMEM((levels, GATE_ROWS, BLOCK), jnp.float32)],
        ),
        out_shape=jax.ShapeDtypeStruct((levels, rows, rows), jnp.bfloat16),
        compiler_params=params("arbitrary", "arbitrary"),
        cost_estimate=pl.CostEstimate(
            flops=2 * 3 * 512 * count * BLOCK * BLOCK * radial_weight.shape[0],
            bytes_accessed=2 * 4 * count * BLOCK * BLOCK,
            transcendentals=count * BLOCK * BLOCK * radial_weight.shape[0],
        ),
        name="gate",
    )(pairs, mask, dist, weights)


def product_kernel(left_ref, right_ref, out_ref):
    out_ref[...] = jnp.dot(
        left_ref[...], right_ref[...], preferred_element_type=jnp.float32
    ).astype(jnp.bfloat16)


def degree_products(left, right):
    width = left.shape[1]
    block = pl.BlockSpec((width, width), lambda i: (i, 0))
    return pl.pallas_call(
        product_kernel,
        grid=(left.shape[0] // width,),
        in_specs=[block, block],
        out_specs=block,
        out_shape=jax.ShapeDtypeStruct(left.shape, jnp.bfloat16),
        compiler_params=params("arbitrary"),
        name="degree_products",
    )(left, right)


def flip_kernel(rows_ref, out_ref):
    out_ref[...] = rows_ref[...].T


def flip_cotangent(cotangent, width, level):
    rows = cotangent.shape[0]
    first, last = span((level,))
    return pl.pallas_call(
        flip_kernel,
        grid=(last - first,),
        in_specs=[pl.BlockSpec((rows, width), lambda i: (0, first + i))],
        out_specs=pl.BlockSpec((width, rows), lambda i: (0, i)),
        out_shape=jax.ShapeDtypeStruct((width, (last - first) * rows), jnp.bfloat16),
        compiler_params=params("arbitrary"),
        name="flip_cotangent",
    )(cotangent)


def outer_kernel(place_ref, gate_ref, local_ref, *refs, pieces, levels):
    cots = refs[: len(levels)]
    near_ref, far_ref, mixed_ref, sum_ref = refs[len(levels) :]
    rows, width = local_ref.shape[0], mixed_ref.shape[1]
    comps = comps_of(levels)
    for slot, level in enumerate(levels):
        first, last = span((level,))
        for comp in range(first, last):
            at = comps.index(comp) * width
            mixed_ref[(comp - first) * rows : (comp - first + 1) * rows, :] = jnp.dot(
                gate_ref[level], local_ref[:, at : at + width], preferred_element_type=jnp.float32
            ).astype(jnp.bfloat16)
        depth = (last - first) * rows
        flipped = jnp.dot(
            cots[slot][...], mixed_ref[0:depth, :], preferred_element_type=jnp.float32
        )
        sum_ref[slot * width : (slot + 1) * width, :] = flipped.T
    half, height = pieces // 2, width // pieces
    for step in range(half):
        near = pl.multiple_of((place_ref[0] ^ step) * height, height)
        far = pl.multiple_of((place_ref[0] ^ (step + half)) * height, height)
        for slot in range(len(levels)):
            to = (step * len(levels) + slot) * height
            near_ref[to : to + height, :] = sum_ref[pl.ds(slot * width + near, height), :]
            far_ref[to : to + height, :] = sum_ref[pl.ds(slot * width + far, height), :].astype(
                jnp.bfloat16
            )


def outer_sum(place, gate, local, cots, width, levels, pieces):
    rows = gate.shape[1]
    whole = len(levels) * width
    deepest = 2 * max(levels) + 1
    total = sum(2 * level + 1 for level in levels)
    return pl.pallas_call(
        functools.partial(outer_kernel, pieces=pieces, levels=levels),
        in_specs=[SCALARS] + [WHOLE] * (2 + len(levels)),
        out_specs=[WHOLE] * 2,
        out_shape=[
            jax.ShapeDtypeStruct((whole // 2, width), jnp.float32),
            jax.ShapeDtypeStruct((whole // 2, width), jnp.bfloat16),
        ],
        scratch_shapes=[
            pltpu.VMEM((deepest * rows, width), jnp.bfloat16),
            pltpu.VMEM((whole, width), jnp.float32),
        ],
        compiler_params=params(),
        cost_estimate=pl.CostEstimate(
            flops=2 * total * rows * width * (rows + width),
            bytes_accessed=4 * total * rows * width,
            transcendentals=0,
        ),
        name="outer_sum",
    )(place, gate, local, *[cots[level] for level in levels])


def update_kernel(gate_ref, map_ref, local_ref, *refs, degrees):
    out_ref, ready_ref, sems = refs[-3:]
    width = map_ref.shape[1]
    copies = []
    for index, comp in enumerate(comps_of(degrees)):
        level = math.isqrt(comp)
        at = index * width
        hidden = local_ref[:, at : at + width]
        mixed = jnp.dot(gate_ref[level], hidden, preferred_element_type=jnp.float32)
        weight = map_ref[level * width : (level + 1) * width, :]
        added = jnp.dot(mixed.astype(jnp.bfloat16), weight, preferred_element_type=jnp.float32)
        ready_ref[index] = (hidden.astype(jnp.float32) + added).astype(jnp.bfloat16)
        copies.append(
            pltpu.make_async_copy(
                ready_ref.at[index],
                out_ref.at[:, pl.ds(comp * width, width)],
                sems.at[index],
            )
        )
        copies[-1].start()
    for copy in copies:
        copy.wait()


def update(gate, maps, local, width, degrees, total, held):
    rows = local.shape[0]
    count = len(comps_of(degrees))
    in_specs = [WHOLE] * 3
    operands = [gate, maps, local]
    aliases = {}
    if held is not None:
        in_specs.append(ANY)
        operands.append(held)
        aliases = {3: 0}
    return pl.pallas_call(
        functools.partial(update_kernel, degrees=degrees),
        in_specs=in_specs,
        out_specs=ANY,
        out_shape=jax.ShapeDtypeStruct((rows, total), jnp.bfloat16),
        scratch_shapes=[
            pltpu.VMEM((count, rows, width), jnp.bfloat16),
            pltpu.SemaphoreType.DMA((count,)),
        ],
        input_output_aliases=aliases,
        compiler_params=params(),
        cost_estimate=pl.CostEstimate(
            flops=2 * count * rows * width * (rows + width),
            bytes_accessed=4 * count * rows * width,
            transcendentals=0,
        ),
        name="update",
    )(*operands)


def place_parts(place_ref, parts, outer_ref):
    width = outer_ref.shape[1]
    height = width // len(parts)
    for step, part in enumerate(parts):
        row = pl.multiple_of((place_ref[0] ^ step) * height, height)
        for slot in range(part.shape[0] // height):
            outer_ref[pl.ds(slot * width + row, height), :] = part[
                slot * height : (slot + 1) * height, :
            ]


def gradients(rows, outer, flipped, weight):
    mix = jnp.dot(rows, weight, preferred_element_type=jnp.float32)
    return mix, jnp.dot(flipped, outer, preferred_element_type=jnp.float32)


def most_kernel(place_ref, weight_ref, flip_ref, *refs, piece):
    *parts, mix_ref, out_ref, outer_ref = refs
    width = weight_ref.shape[0]

    @pl.when(pl.program_id(0) == 0)
    def _():
        place_parts(place_ref, parts, outer_ref)

    row = (place_ref[1] + pl.program_id(0)) * piece

    @pl.when(row < len(MOST) * width)
    def _():
        first = pl.multiple_of((row // width - place_ref[2]) * width, width)
        mix_ref[...], out_ref[...] = gradients(
            outer_ref[pl.ds(pl.multiple_of(first + row % width, piece), piece), :],
            outer_ref[pl.ds(first, width), :],
            flip_ref[...],
            weight_ref[...],
        )


def most_gradients(place, weight, flipped, parts, shard, piece):
    width = weight.shape[1]
    whole = pl.BlockSpec(parts[0].shape, lambda i, place: (0, 0))
    return pl.pallas_call(
        functools.partial(most_kernel, piece=piece),
        grid_spec=pltpu.PrefetchScalarGridSpec(
            num_scalar_prefetch=1,
            grid=(shard // piece,),
            in_specs=[
                pl.BlockSpec(
                    (width, width), lambda i, place: ((place[1] + i) * piece // width, 0)
                ),
                pl.BlockSpec((piece, width), lambda i, place: (place[1] + i, 0)),
            ]
            + [whole] * len(parts),
            out_specs=[pl.BlockSpec((piece, width), lambda i, place: (i, 0))] * 2,
            scratch_shapes=[pltpu.VMEM((len(parts) * parts[0].shape[0], width), jnp.bfloat16)],
        ),
        out_shape=[jax.ShapeDtypeStruct((shard, width), jnp.float32)] * 2,
        compiler_params=params("arbitrary", limit=GRADIENT_LIMIT),
        name="most_gradients",
    )(place, weight, flipped, *parts)


def last_kernel(place_ref, weight_ref, flip_ref, *refs, piece):
    *parts, _, _, mix_out, out_out, outer_ref, mix_ref, out_ref, sems = refs
    width = weight_ref.shape[0]
    place_parts(place_ref, parts, outer_ref)
    count = mix_ref.shape[0]

    def each(index):
        row = (place_ref[1] + index) * piece - LAST[0] * width
        to = pl.ds(index * piece, piece)
        copies = [
            pltpu.make_async_copy(mix_ref.at[index], mix_out.at[to, :], sems.at[index, 0]),
            pltpu.make_async_copy(out_ref.at[index], out_out.at[to, :], sems.at[index, 1]),
        ]
        return row, (row >= 0) & (row < width), copies

    for index in range(count):
        row, held, copies = each(index)

        @pl.when(held)
        def _():
            mine = pl.ds(pl.multiple_of(row, piece), piece)
            mix_ref[index], out_ref[index] = gradients(
                outer_ref[mine, :], outer_ref[...], flip_ref[mine, :], weight_ref[...]
            )
            for copy in copies:
                copy.start()

    for index in range(count):
        _, held, copies = each(index)

        @pl.when(held)
        def _():
            for copy in copies:
                copy.wait()


def last_gradients(place, weight, flipped, parts, mix_grad, out_grad, piece):
    shard, width = mix_grad.shape
    own = pl.BlockSpec((width, width), lambda i: (LAST[0], 0))
    whole = pl.BlockSpec(parts[0].shape, lambda i: (0, 0))
    count = shard // piece
    return pl.pallas_call(
        functools.partial(last_kernel, piece=piece),
        grid=(1,),
        in_specs=[SCALARS, own, own] + [whole] * len(parts) + [ANY] * 2,
        out_specs=[ANY] * 2,
        out_shape=[jax.ShapeDtypeStruct(mix_grad.shape, jnp.float32)] * 2,
        scratch_shapes=[
            pltpu.VMEM((width, width), jnp.bfloat16),
            pltpu.VMEM((count, piece, width), jnp.float32),
            pltpu.VMEM((count, piece, width), jnp.float32),
            pltpu.SemaphoreType.DMA((count, 2)),
        ],
        input_output_aliases={3 + len(parts): 0, 4 + len(parts): 1},
        compiler_params=params("arbitrary", limit=GRADIENT_LIMIT),
        name="last_gradients",
    )(place, weight, flipped, *parts, mix_grad, out_grad)


def body(
    features,
    cotangent,
    send_order,
    pair_index,
    edge_mask,
    distance,
    radial_weight,
    mix_weight,
    out_weight,
    *,
    n_dp,
    n_blk,
):
    rows, total = features.shape
    width = mix_weight.shape[1]
    pieces = 2 * n_blk
    shard = mix_weight.shape[0] // n_blk
    piece = math.gcd(shard, width)
    at_dp, at_blk = lax.axis_index("dp"), lax.axis_index("blk")
    reach = max(((i + 1) * shard - 1) // width - i * shard // width + 1 for i in range(n_blk))
    reach = min(reach, len(MOST))

    def first_degree(at):
        return jnp.minimum(at * shard // width, len(MOST) - reach)

    place = jnp.stack(
        [at_dp % 2 * n_blk + at_blk, at_blk * (shard // piece), first_degree(at_blk)]
    ).astype(jnp.int32)

    def over_dp(value, step):
        return lax.ppermute(value, "dp", [(i, i ^ step) for i in range(n_dp)])

    def over_blk(value, step):
        return lax.ppermute(value, "blk", [(i, i ^ step) for i in range(n_blk)])

    def all_to_all(value):
        return lax.all_to_all(value, "dp", split_axis=0, concat_axis=0, tiled=True)

    def chip_sum(near, far):
        return near + over_dp(far, 1).astype(jnp.float32)

    def plane_sum(chip):
        height = chip.shape[0] // n_blk
        own = chip[:height]
        for step in range(1, n_blk):
            part = chip[step * height : (step + 1) * height].astype(jnp.bfloat16)
            own = own + over_blk(part, step).astype(jnp.float32)
        return own

    bits = [1 << i for i in range((n_dp // 2).bit_length() - 1)]
    upper = [(at_dp // 2) & bit for bit in bits]

    def z_halved(own):
        for bit, high in zip(bits[:-1], upper):
            half = own.shape[0] // 2
            kept = jnp.where(high > 0, own[half:], own[:half])
            given = jnp.where(high > 0, own[:half], own[half:]).astype(jnp.bfloat16)
            own = kept + over_dp(given, 2 * bit).astype(jnp.float32)
        own = own.astype(jnp.bfloat16)
        return own, over_dp(own, 2 * bits[-1])

    def z_joined(own, *others):
        for bit, high in reversed(list(zip(bits[:-1], upper))):
            other = after(over_dp(own, 2 * bit), *others)
            own = jnp.where(
                high > 0,
                jnp.concatenate([other, own], axis=0),
                jnp.concatenate([own, other], axis=0),
            )
        return own

    def plane_gather(own, needed, *others):
        near = [needed(own, at_blk)]
        near += [over_blk(needed(own, at_blk ^ step), step) for step in range(1, n_blk)]
        return near + [over_dp(after(part, *others), 1) for part in near]

    def needed_degrees(own, at):
        height = width // pieces
        return lax.dynamic_slice_in_dim(own, first_degree(at) * height, reach * height, axis=0)

    sent_most = pick_rows(send_order, features, width, MOST)
    came_most = all_to_all(sent_most)
    sent_last = pick_rows(send_order, after(features, sent_most), width, LAST)
    gate = gate_matrices(pair_index, edge_mask, after(distance, sent_last), radial_weight, rows)
    cotangent, mix_weight, out_weight = lax.optimization_barrier(
        (cotangent, mix_weight, out_weight, gate)
    )[:3]
    cots = {level: flip_cotangent(cotangent, width, level) for level in MOST + LAST}
    maps = degree_products(mix_weight, out_weight)
    flipped, out_flipped = (
        weight.reshape(LMAX + 1, width, width).swapaxes(1, 2).reshape(weight.shape)
        for weight in (mix_weight, out_weight)
    )
    ready = (gate, maps, flipped, out_flipped, *cots.values())
    came_last = all_to_all(after(sent_last, came_most, *ready))

    local = after(came_most, *ready)
    own = plane_sum(chip_sum(*outer_sum(place, gate, local, cots, width, MOST, pieces)))
    own, other = z_halved(own)
    updated = update(gate, maps, local, width, MOST, total, None)

    local = after(came_last, own, other, updated)
    near, far = outer_sum(place, gate, local, cots, width, LAST, pieces)
    most = tree_sum([own, after(other, near)])
    last = plane_sum(chip_sum(near, far)).astype(jnp.bfloat16)
    local = after(local, last)
    others = [over_dp(last, 2 * step) for step in range(1, n_dp // 2)]
    updated = update(gate, maps, local, width, LAST, total, updated)
    *others, updated = lax.optimization_barrier((*others, updated))
    last = tree_sum([last, *others])
    most = plane_gather(z_joined(most, *others), needed_degrees)
    mix_grad, out_grad = most_gradients(place, out_flipped, flipped, most, shard, piece)
    last = plane_gather(after(last, updated), lambda own, at: own, mix_grad)
    mix_grad, out_grad = last_gradients(
        place, out_flipped, flipped, last, mix_grad, out_grad, piece
    )
    return updated, mix_grad, out_grad


def solution(mesh):
    in_specs = (
        P(("dp", "blk"), None),
        P(("dp", "blk"), None),
        P(("dp", "blk"), None),
        P(("dp", "blk"), None),
        P(("dp", "blk"), None, None),
        P(("dp", "blk"), None, None),
        P(),
        P(),
        P(),
    )
    out_specs = (P(("dp", "blk"), None), P("blk", None), P("blk", None))
    run = functools.partial(body, n_dp=mesh.shape["dp"], n_blk=mesh.shape["blk"])
    return jax.shard_map(run, mesh=mesh, in_specs=in_specs, out_specs=out_specs, check_vma=False)
```

profile of v0, /device:TPU:0, one launch (start us, length us, event | category | flops | bytes accessed | tf_op | source)
XLA Modules:
  0.0 217.0 jit_solution(15628692204359367794)
XLA Ops:
  0.6 4.6 %pick_rows.2 = bf16[256,8192]{1,0:T(8,128)(2,1)} custom-call(s32[1,256]{1,0:T(1,128)} %order_ref.3, bf16[256,12800]{1,0:T(8,128)(2,1)} %rows_ref.2), custom_call_target="tpu_custom_call" | custom-call | tf_op jit(solution)/shard_map/pick_rows/pallas_call | solution.py:94
  5.3 6.3 %all-to-all-start = ((bf16[8,32,8192]{2,1,0:T(8,128)(2,1)}), bf16[8,32,8192]{2,1,0:T(8,128)(2,1)}, u32[]{:S(2)}, u32[]{:S(2)}) async-start(bf16[8,32,8192]{2,1,0:T(8,128)(2,1)} %bitcast.26), calls=%async_computation | async-start | bytes 8388608 | tf_op jit(solution)/shard_map/all_to_all | solution.py:483
  11.7 3.4 %pick_rows.3 = bf16[256,4608]{1,0:T(8,128)(2,1)} custom-call(s32[1,256]{1,0:T(1,128)} %order_ref.3, bf16[256,12800]{1,0:T(8,128)(2,1)} %rows_ref.2), custom_call_target="tpu_custom_call" | custom-call | tf_op jit(solution)/shard_map/pick_rows/pallas_call | solution.py:94
  15.2 32.0 %gate.1.gate_ref = bf16[5,256,256]{2,1,0:T(8,128)(2,1)S(1)} custom-call(s32[3,2]{1,0:T(4,128)S(1)} %copy.15.pairs_ref, s32[3,128,128]{2,1,0:T(8,128)S(1)} %copy-done.14, f32[3,128,128]{2,1,0:T(8,128)S(1)} %copy-done.15, bf16[16,512]{1,0:T(8,128)(2,1)S(1)} %fusion.7.weight_ref), custom_call_target="tpu_custom_call" | custom-call | flops 77309411328 | bytes 393216 | tf_op jit(solution)/shard_map/gate/pallas_call | solution.py:158
  48.4 2.2 %flip_cotangent.6.refs_1_ = bf16[512,768]{1,0:T(8,128)(2,1)S(1)} custom-call(bf16[256,12800]{1,0:T(8,128)(2,1)} %rows_ref.7), custom_call_target="tpu_custom_call" | custom-call | tf_op jit(solution)/shard_map/flip_cotangent/pallas_call | solution.py:205
  51.5 3.3 %flip_cotangent.7.refs_2_ = bf16[512,1280]{1,0:T(8,128)(2,1)S(1)} custom-call(bf16[256,12800]{1,0:T(8,128)(2,1)} %rows_ref.7), custom_call_target="tpu_custom_call" | custom-call | tf_op jit(solution)/shard_map/flip_cotangent/pallas_call | solution.py:205
  55.8 4.4 %flip_cotangent.8.refs_3_ = bf16[512,1792]{1,0:T(8,128)(2,1)S(1)} custom-call(bf16[256,12800]{1,0:T(8,128)(2,1)} %rows_ref.7), custom_call_target="tpu_custom_call" | custom-call | tf_op jit(solution)/shard_map/flip_cotangent/pallas_call | solution.py:205
  61.5 5.7 %flip_cotangent.9.refs_0_ = bf16[512,2304]{1,0:T(8,128)(2,1)S(1)} custom-call(bf16[256,12800]{1,0:T(8,128)(2,1)} %rows_ref.7), custom_call_target="tpu_custom_call" | custom-call | tf_op jit(solution)/shard_map/flip_cotangent/pallas_call | solution.py:205
  68.6 4.5 %degree_products.1.map_ref = bf16[2560,512]{1,0:T(8,128)(2,1)S(1)} custom-call(bf16[2560,512]{1,0:T(8,128)(2,1)S(1)} %copy-done.4, bf16[2560,512]{1,0:T(8,128)(2,1)} %right_ref), custom_call_target="tpu_custom_call" | custom-call | tf_op jit(solution)/shard_map/degree_products/pallas_call | solution.py:187
  74.7 3.0 %copy.17 = bf16[5,512,512]{1,2,0:T(8,128)(2,1)S(1)} copy(bf16[5,512,512]{2,1,0:T(8,128)(2,1)} %bitcast.27) | data formatting | bytes 5242880 | tf_op jit(solution)/shard_map/reshape | solution.py:537
  77.6 4.4 %copy.16 = bf16[5,512,512]{1,2,0:T(8,128)(2,1)} copy(bf16[5,512,512]{2,1,0:T(8,128)(2,1)} %bitcast.25) | data formatting | bytes 5242880 | tf_op jit(solution)/shard_map/reshape | solution.py:537
  82.1 23.7 %all-to-all-done = bf16[8,32,8192]{2,1,0:T(8,128)(2,1)} async-done(((bf16[8,32,8192]{2,1,0:T(8,128)(2,1)}), bf16[8,32,8192]{2,1,0:T(8,128)(2,1)}, u32[]{:S(2)}, u32[]{:S(2)}) %all-to-all-start) | async-done | bytes 4194336 | tf_op jit(solution)/shard_map/all_to_all | solution.py:483
  105.7 4.6 %all-to-all-start.1 = ((bf16[8,32,4608]{2,1,0:T(8,128)(2,1)}), bf16[8,32,4608]{2,1,0:T(8,128)(2,1)}, u32[]{:S(2)}, u32[]{:S(2)}) async-start(bf16[8,32,4608]{2,1,0:T(8,128)(2,1)} %bitcast.28), calls=%async_computation.1 | async-start | bytes 4718592 | tf_op jit(solution)/shard_map/all_to_all | solution.py:483
  114.4 7.6 %outer_sum.2 = (f32[1024,512]{1,0:T(8,128)}, bf16[1024,512]{1,0:T(8,128)(2,1)S(1)}) custom-call(s32[3]{0:T(128)S(1)} %pad_add_fusion.place_ref, bf16[5,256,256]{2,1,0:T(8,128)(2,1)S(1)} %gate.1.gate_ref, bf16[256,8192]{1,0:T(8,128)(2,1)} %bitcast.5.local_ref, bf16[512,256]{1,0:T(8,128)(2,1)S(1)} %flip_cotangent.5.refs_0_, bf16[512,768]{1,0:T(8,128)(2,1)S(1)} %copy-done.12, ...), custom_call_target="tpu_custom_call" | custom-call | flops 3221225472 | bytes 8388608 | tf_op jit(solution)/shard_map/outer_sum/pallas_call | solution.py:250
  122.1 2.5 %collective-permute-done = bf16[1024,512]{1,0:T(8,128)(2,1)S(1)} collective-permute-done((bf16[1024,512]{1,0:T(8,128)(2,1)S(1)}, bf16[1024,512]{1,0:T(8,128)(2,1)S(1)}, u32[]{:S(2)}, u32[]{:S(2)}) %collective-permute-start) | collective-permute-done | bytes 1048608 | tf_op jit(solution)/shard_map/ppermute | solution.py:477
  124.6 3.3 %fusion.10 = (bf16[1024,512]{1,0:T(8,128)(2,1)S(1)}, f32[1024,512]{1,0:T(8,128)}) fusion(f32[1024,512]{1,0:T(8,128)} %get-tuple-element.38, bf16[1024,512]{1,0:T(8,128)(2,1)S(1)} %collective-permute-done), kind=kLoop, calls=%fused_computation.28 | loop fusion | flops 1572864 | bytes 6291456 | tf_op jit(solution)/shard_map/convert.5
  132.3 5.9 %collective-permute-done.1 = bf16[256,512]{1,0:T(8,128)(2,1)S(1)} collective-permute-done((bf16[256,512]{1,0:T(8,128)(2,1)}, bf16[256,512]{1,0:T(8,128)(2,1)S(1)}, u32[]{:S(2)}, u32[]{:S(2)}) %collective-permute-start.1) | collective-permute-done | bytes 262176 | tf_op jit(solution)/shard_map/ppermute | solution.py:480
  138.2 6.0 %collective-permute-done.3 = bf16[256,512]{1,0:T(8,128)(2,1)} collective-permute-done((bf16[256,512]{1,0:T(8,128)(2,1)}, bf16[256,512]{1,0:T(8,128)(2,1)}, u32[]{:S(2)}, u32[]{:S(2)}) %collective-permute-start.3) | collective-permute-done | bytes 262176 | tf_op jit(solution)/shard_map/ppermute | solution.py:480
  146.9 1.7 collective-permute-start.4
  148.7 3.3 %collective-permute-done.4 = bf16[128,512]{1,0:T(8,128)(2,1)S(1)} collective-permute-done((bf16[128,512]{1,0:T(8,128)(2,1)S(1)}, bf16[128,512]{1,0:T(8,128)(2,1)S(1)}, u32[]{:S(2)}, u32[]{:S(2)}) %collective-permute-start.4) | collective-permute-done | bytes 131104 | tf_op jit(solution)/shard_map/ppermute | solution.py:477
  152.0 4.5 %collective-permute-start.5 = (bf16[128,512]{1,0:T(8,128)(2,1)S(1)}, bf16[128,512]{1,0:T(8,128)(2,1)}, u32[]{:S(2)}, u32[]{:S(2)}) collective-permute-start(bf16[128,512]{1,0:T(8,128)(2,1)S(1)} %add_convert_fusion.1), channel_id=1, source_target_pairs={{0,16},{4,20},{8,24},{12,28},{16,0},{20,4},{24,8},{28,12},{1,17},{... | collective-permute-start | bytes 393224 | tf_op jit(solution)/shard_map/ppermute | solution.py:477
  156.6 7.9 %update.2.refs_0_ = bf16[256,12800]{1,0:T(8,128)(2,1)} custom-call(bf16[5,256,256]{2,1,0:T(8,128)(2,1)S(1)} %gate.1.gate_ref, bf16[2560,512]{1,0:T(8,128)(2,1)S(1)} %copy-done.2, bf16[256,8192]{1,0:T(8,128)(2,1)} %bitcast.5.local_ref), custom_call_target="tpu_custom_call" | custom-call | flops 3221225472 | bytes 8388608 | tf_op jit(solution)/shard_map/update/pallas_call | solution.py:306
  164.4 6.0 %collective-permute-done.5 = bf16[128,512]{1,0:T(8,128)(2,1)} collective-permute-done((bf16[128,512]{1,0:T(8,128)(2,1)S(1)}, bf16[128,512]{1,0:T(8,128)(2,1)}, u32[]{:S(2)}, u32[]{:S(2)}) %collective-permute-start.5) | collective-permute-done | bytes 131104 | tf_op jit(solution)/shard_map/ppermute | solution.py:477
  170.4 1.7 copy-done.6
  172.1 4.0 %outer_sum.3 = (f32[256,512]{1,0:T(8,128)S(1)}, bf16[256,512]{1,0:T(8,128)(2,1)S(1)}) custom-call(s32[3]{0:T(128)S(1)} %pad_add_fusion.place_ref, bf16[5,256,256]{2,1,0:T(8,128)(2,1)S(1)} %gate.1.gate_ref, bf16[256,4608]{1,0:T(8,128)(2,1)} %bitcast.13.local_ref, bf16[512,2304]{1,0:T(8,128)(2,1)S(1)} %copy-done.6), custom_call_target="tpu_custom_call" | custom-call | flops 1811939328 | bytes 4718592 | tf_op jit(solution)/shard_map/outer_sum/pallas_call | solution.py:250
  176.9 1.7 collective-permute-done.6
  179.7 1.6 collective-permute-start.7
  184.4 2.1 collective-permute-done.9
  189.0 3.1 %collective-permute-start.10 = (bf16[64,512]{1,0:T(8,128)(2,1)S(1)}, bf16[64,512]{1,0:T(8,128)(2,1)S(1)}, u32[]{:S(2)}, u32[]{:S(2)}) collective-permute-start(bf16[64,512]{1,0:T(8,128)(2,1)S(1)} %fusion.4), channel_id=1, source_target_pairs={{0,8},{4,12},{8,0},{12,4},{16,24},{20,28},{24,16},{28,20},{1,9},{5... | collective-permute-start | bytes 196616 | tf_op jit(solution)/shard_map/ppermute | solution.py:477
  192.1 5.6 %update.3 = bf16[256,12800]{1,0:T(8,128)(2,1)} custom-call(bf16[5,256,256]{2,1,0:T(8,128)(2,1)S(1)} %gate.1.gate_ref, bf16[2560,512]{1,0:T(8,128)(2,1)S(1)} %copy-done.3, bf16[256,4608]{1,0:T(8,128)(2,1)} %bitcast.13.local_ref, bf16[256,12800]{1,0:T(8,128)(2,1)} %update.2.refs_0_), custom_call_target="tpu_custom_call", output_to_operand_aliasing={{}: (3, {})} | custom-call | flops 1811939328 | bytes 4718592 | tf_op jit(solution)/shard_map/update/pallas_call | solution.py:306
  201.5 3.2 %collective-permute-done.19.refs_3_ = bf16[128,512]{1,0:T(8,128)(2,1)S(1)} collective-permute-done((bf16[128,512]{1,0:T(8,128)(2,1)S(1)}, bf16[128,512]{1,0:T(8,128)(2,1)S(1)}, u32[]{:S(2)}, u32[]{:S(2)}) %collective-permute-start.19) | collective-permute-done | bytes 131104 | tf_op jit(solution)/shard_map/ppermute | solution.py:480
  210.1 4.0 %most_gradients.1 = (f32[640,512]{1,0:T(8,128)}, f32[640,512]{1,0:T(8,128)}) custom-call(s32[3]{0:T(128)S(1)} %pad_add_fusion.place_ref, bf16[2560,512]{1,0:T(8,128)(2,1)S(1)} %bitcast.21, bf16[2560,512]{1,0:T(8,128)(2,1)S(1)} %bitcast.23, bf16[128,512]{1,0:T(8,128)(2,1)S(1)} %get-tuple-element.71.refs_0_, ...), custom_call_target="tpu_custom_call" | custom-call | tf_op jit(solution)/shard_map/most_gradients/pallas_call | solution.py:366
  (99 shorter events, 38.0 us)
Async XLA Ops:
  5.3 100.5 %all-to-all-start = ((bf16[8,32,8192]{2,1,0:T(8,128)(2,1)}), bf16[8,32,8192]{2,1,0:T(8,128)(2,1)}, u32[]{:S(2)}, u32[]{:S(2)}) async-start(bf16[8,32,8192]{2,1,0:T(8,128)(2,1)} %bitcast.26), calls=%async_computation | async-start | bytes 8388608 | tf_op jit(solution)/shard_map/all_to_all | solution.py:483
  105.7 64.7 %all-to-all-start.1 = ((bf16[8,32,4608]{2,1,0:T(8,128)(2,1)}), bf16[8,32,4608]{2,1,0:T(8,128)(2,1)}, u32[]{:S(2)}, u32[]{:S(2)}) async-start(bf16[8,32,4608]{2,1,0:T(8,128)(2,1)} %bitcast.28), calls=%async_computation.1 | async-start | bytes 4718592 | tf_op jit(solution)/shard_map/all_to_all | solution.py:483
  121.9 2.7 %collective-permute-start = (bf16[1024,512]{1,0:T(8,128)(2,1)S(1)}, bf16[1024,512]{1,0:T(8,128)(2,1)S(1)}, u32[]{:S(2)}, u32[]{:S(2)}) collective-permute-start(bf16[1024,512]{1,0:T(8,128)(2,1)S(1)} %get-tuple-element.39), channel_id=1, source_target_pairs={{0,4},{4,0},{8,12},{12,8},{16,20},{20,16},{24,28},{28,24},{1,5},{5... | collective-permute-start | bytes 3145736 | tf_op jit(solution)/shard_map/ppermute | solution.py:477
  128.8 9.4 %collective-permute-start.1 = (bf16[256,512]{1,0:T(8,128)(2,1)}, bf16[256,512]{1,0:T(8,128)(2,1)S(1)}, u32[]{:S(2)}, u32[]{:S(2)}) collective-permute-start(bf16[256,512]{1,0:T(8,128)(2,1)} %get-tuple-element.65), channel_id=1, source_target_pairs={{0,1},{1,0},{2,3},{3,2},{4,5},{5,4},{6,7},{7,6},{8,9},{9,8},{10,11... | collective-permute-start | bytes 786440 | tf_op jit(solution)/shard_map/ppermute | solution.py:480
  130.3 13.9 %collective-permute-start.3 = (bf16[256,512]{1,0:T(8,128)(2,1)}, bf16[256,512]{1,0:T(8,128)(2,1)}, u32[]{:S(2)}, u32[]{:S(2)}) collective-permute-start(bf16[256,512]{1,0:T(8,128)(2,1)} %get-tuple-element.66), channel_id=1, source_target_pairs={{0,3},{1,2},{2,1},{3,0},{4,7},{5,6},{6,5},{7,4},{8,11},{9,10},{10,... | collective-permute-start | bytes 786440 | tf_op jit(solution)/shard_map/ppermute | solution.py:480
  131.8 13.7 %collective-permute-start.2 = (bf16[256,512]{1,0:T(8,128)(2,1)}, bf16[256,512]{1,0:T(8,128)(2,1)}, u32[]{:S(2)}, u32[]{:S(2)}) collective-permute-start(bf16[256,512]{1,0:T(8,128)(2,1)} %get-tuple-element.67), channel_id=1, source_target_pairs={{0,2},{1,3},{2,0},{3,1},{4,6},{5,7},{6,4},{7,5},{8,10},{9,11},{10,... | collective-permute-start | bytes 786440 | tf_op jit(solution)/shard_map/ppermute | solution.py:480
  132.3 24.2 %copy-start.2 = (bf16[2560,512]{1,0:T(8,128)(2,1)S(1)}, bf16[2560,512]{1,0:T(8,128)(2,1)}, u32[]{:S(2)}) copy-start(bf16[2560,512]{1,0:T(8,128)(2,1)} %copy-done.1) | copy-start | bytes 7864324
  146.9 5.0 %collective-permute-start.4 = (bf16[128,512]{1,0:T(8,128)(2,1)S(1)}, bf16[128,512]{1,0:T(8,128)(2,1)S(1)}, u32[]{:S(2)}, u32[]{:S(2)}) collective-permute-start(bf16[128,512]{1,0:T(8,128)(2,1)S(1)} %select_convert_fusion), channel_id=1, source_target_pairs={{0,8},{4,12},{8,0},{12,4},{16,24},{20,28},{24,16},{28,20},{1,9},{5... | collective-permute-start | bytes 393224 | tf_op jit(solution)/shard_map/ppermute | solution.py:477
  152.0 18.4 %collective-permute-start.5 = (bf16[128,512]{1,0:T(8,128)(2,1)S(1)}, bf16[128,512]{1,0:T(8,128)(2,1)}, u32[]{:S(2)}, u32[]{:S(2)}) collective-permute-start(bf16[128,512]{1,0:T(8,128)(2,1)S(1)} %add_convert_fusion.1), channel_id=1, source_target_pairs={{0,16},{4,20},{8,24},{12,28},{16,0},{20,4},{24,8},{28,12},{1,17},{... | collective-permute-start | bytes 393224 | tf_op jit(solution)/shard_map/ppermute | solution.py:477
  176.9 1.7 collective-permute-start.6
  179.7 4.6 %collective-permute-start.7 = (bf16[64,512]{1,0:T(8,128)(2,1)S(1)}, bf16[64,512]{1,0:T(8,128)(2,1)S(1)}, u32[]{:S(2)}, u32[]{:S(2)}) collective-permute-start(bf16[64,512]{1,0:T(8,128)(2,1)S(1)} %get-tuple-element.72), channel_id=1, source_target_pairs={{0,1},{1,0},{2,3},{3,2},{4,5},{5,4},{6,7},{7,6},{8,9},{9,8},{10,11... | collective-permute-start | bytes 196616 | tf_op jit(solution)/shard_map/ppermute | solution.py:480
  181.3 5.2 %collective-permute-start.9 = (bf16[64,512]{1,0:T(8,128)(2,1)S(1)}, bf16[64,512]{1,0:T(8,128)(2,1)S(1)}, u32[]{:S(2)}, u32[]{:S(2)}) collective-permute-start(bf16[64,512]{1,0:T(8,128)(2,1)S(1)} %get-tuple-element.73), channel_id=1, source_target_pairs={{0,3},{1,2},{2,1},{3,0},{4,7},{5,6},{6,5},{7,4},{8,11},{9,10},{10,... | collective-permute-start | bytes 196616 | tf_op jit(solution)/shard_map/ppermute | solution.py:480
  182.8 4.8 %collective-permute-start.8 = (bf16[64,512]{1,0:T(8,128)(2,1)S(1)}, bf16[64,512]{1,0:T(8,128)(2,1)S(1)}, u32[]{:S(2)}, u32[]{:S(2)}) collective-permute-start(bf16[64,512]{1,0:T(8,128)(2,1)S(1)} %get-tuple-element.74), channel_id=1, source_target_pairs={{0,2},{1,3},{2,0},{3,1},{4,6},{5,7},{6,4},{7,5},{8,10},{9,11},{10,... | collective-permute-start | bytes 196616 | tf_op jit(solution)/shard_map/ppermute | solution.py:480
  184.3 13.5 %collective-permute-start.16 = (bf16[128,512]{1,0:T(8,128)(2,1)S(1)}, bf16[128,512]{1,0:T(8,128)(2,1)S(1)}, u32[]{:S(2)}, u32[]{:S(2)}) collective-permute-start(bf16[128,512]{1,0:T(8,128)(2,1)S(1)} %add_convert_fusion), channel_id=1, source_target_pairs={{0,8},{4,12},{8,0},{12,4},{16,24},{20,28},{24,16},{28,20},{1,9},{5... | collective-permute-start | bytes 393224 | tf_op jit(solution)/shard_map/ppermute | solution.py:477
  187.7 10.1 %collective-permute-start.12 = (bf16[64,512]{1,0:T(8,128)(2,1)S(1)}, bf16[64,512]{1,0:T(8,128)(2,1)S(1)}, u32[]{:S(2)}, u32[]{:S(2)}) collective-permute-start(bf16[64,512]{1,0:T(8,128)(2,1)S(1)} %fusion.4), channel_id=1, source_target_pairs={{0,24},{4,28},{8,16},{12,20},{16,8},{20,12},{24,0},{28,4},{1,25},{... | collective-permute-start | bytes 196616 | tf_op jit(solution)/shard_map/ppermute | solution.py:477
  189.0 8.8 %collective-permute-start.11 = (bf16[64,512]{1,0:T(8,128)(2,1)S(1)}, bf16[64,512]{1,0:T(8,128)(2,1)S(1)}, u32[]{:S(2)}, u32[]{:S(2)}) collective-permute-start(bf16[64,512]{1,0:T(8,128)(2,1)S(1)} %fusion.4), channel_id=1, source_target_pairs={{0,16},{4,20},{8,24},{12,28},{16,0},{20,4},{24,8},{28,12},{1,17},{... | collective-permute-start | bytes 196616 | tf_op jit(solution)/shard_map/ppermute | solution.py:477
  189.0 8.8 %collective-permute-start.10 = (bf16[64,512]{1,0:T(8,128)(2,1)S(1)}, bf16[64,512]{1,0:T(8,128)(2,1)S(1)}, u32[]{:S(2)}, u32[]{:S(2)}) collective-permute-start(bf16[64,512]{1,0:T(8,128)(2,1)S(1)} %fusion.4), channel_id=1, source_target_pairs={{0,8},{4,12},{8,0},{12,4},{16,24},{20,28},{24,16},{28,20},{1,9},{5... | collective-permute-start | bytes 196616 | tf_op jit(solution)/shard_map/ppermute | solution.py:477
  192.1 18.0 %copy-start = (bf16[5,512,512]{1,2,0:T(8,128)(2,1)S(1)}, bf16[5,512,512]{1,2,0:T(8,128)(2,1)}, u32[]{:S(2)}) copy-start(bf16[5,512,512]{1,2,0:T(8,128)(2,1)} %copy.16) | copy-start | bytes 7864324
  197.9 6.8 %collective-permute-start.19 = (bf16[128,512]{1,0:T(8,128)(2,1)S(1)}, bf16[128,512]{1,0:T(8,128)(2,1)S(1)}, u32[]{:S(2)}, u32[]{:S(2)}) collective-permute-start(bf16[128,512]{1,0:T(8,128)(2,1)S(1)} %get-tuple-element.68), channel_id=1, source_target_pairs={{0,3},{1,2},{2,1},{3,0},{4,7},{5,6},{6,5},{7,4},{8,11},{9,10},{10,... | collective-permute-start | bytes 393224 | tf_op jit(solution)/shard_map/ppermute | solution.py:480
  199.3 6.6 %collective-permute-start.18 = (bf16[128,512]{1,0:T(8,128)(2,1)S(1)}, bf16[128,512]{1,0:T(8,128)(2,1)S(1)}, u32[]{:S(2)}, u32[]{:S(2)}) collective-permute-start(bf16[128,512]{1,0:T(8,128)(2,1)S(1)} %get-tuple-element.69), channel_id=1, source_target_pairs={{0,2},{1,3},{2,0},{3,1},{4,6},{5,7},{6,4},{7,5},{8,10},{9,11},{10,... | collective-permute-start | bytes 393224 | tf_op jit(solution)/shard_map/ppermute | solution.py:480
  200.6 5.4 %collective-permute-start.17 = (bf16[128,512]{1,0:T(8,128)(2,1)S(1)}, bf16[128,512]{1,0:T(8,128)(2,1)S(1)}, u32[]{:S(2)}, u32[]{:S(2)}) collective-permute-start(bf16[128,512]{1,0:T(8,128)(2,1)S(1)} %get-tuple-element.70), channel_id=1, source_target_pairs={{0,1},{1,0},{2,3},{3,2},{4,5},{5,4},{6,7},{7,6},{8,9},{9,8},{10,11... | collective-permute-start | bytes 393224 | tf_op jit(solution)/shard_map/ppermute | solution.py:480
  201.5 6.5 %collective-permute-start.20 = (bf16[128,512]{1,0:T(8,128)(2,1)S(1)}, bf16[128,512]{1,0:T(8,128)(2,1)S(1)}, u32[]{:S(2)}, u32[]{:S(2)}) collective-permute-start(bf16[128,512]{1,0:T(8,128)(2,1)S(1)} %get-tuple-element.71.refs_0_), channel_id=1, source_target_pairs={{0,4},{4,0},{8,12},{12,8},{16,20},{20,16},{24,28},{28,24},{1,5},{5... | collective-permute-start | bytes 393224 | tf_op jit(solution)/shard_map/ppermute | solution.py:477
  204.7 4.0 %collective-permute-start.23 = (bf16[128,512]{1,0:T(8,128)(2,1)S(1)}, bf16[128,512]{1,0:T(8,128)(2,1)S(1)}, u32[]{:S(2)}, u32[]{:S(2)}) collective-permute-start(bf16[128,512]{1,0:T(8,128)(2,1)S(1)} %collective-permute-done.19.refs_3_), channel_id=1, source_target_pairs={{0,4},{4,0},{8,12},{12,8},{16,20},{20,16},{24,28},{28,24},{1,5},{5... | collective-permute-start | bytes 393224 | tf_op jit(solution)/shard_map/ppermute | solution.py:477
  206.0 4.1 %collective-permute-start.22 = (bf16[128,512]{1,0:T(8,128)(2,1)S(1)}, bf16[128,512]{1,0:T(8,128)(2,1)S(1)}, u32[]{:S(2)}, u32[]{:S(2)}) collective-permute-start(bf16[128,512]{1,0:T(8,128)(2,1)S(1)} %collective-permute-done.18.refs_2_), channel_id=1, source_target_pairs={{0,4},{4,0},{8,12},{12,8},{16,20},{20,16},{24,28},{28,24},{1,5},{5... | collective-permute-start | bytes 393224 | tf_op jit(solution)/shard_map/ppermute | solution.py:477
  206.0 4.1 %collective-permute-start.21 = (bf16[128,512]{1,0:T(8,128)(2,1)S(1)}, bf16[128,512]{1,0:T(8,128)(2,1)S(1)}, u32[]{:S(2)}, u32[]{:S(2)}) collective-permute-start(bf16[128,512]{1,0:T(8,128)(2,1)S(1)} %collective-permute-done.17.refs_1_), channel_id=1, source_target_pairs={{0,4},{4,0},{8,12},{12,8},{16,20},{20,16},{24,28},{28,24},{1,5},{5... | collective-permute-start | bytes 393224 | tf_op jit(solution)/shard_map/ppermute | solution.py:477
  206.5 7.5 %collective-permute-start.15 = (bf16[64,512]{1,0:T(8,128)(2,1)S(1)}, bf16[64,512]{1,0:T(8,128)(2,1)S(1)}, u32[]{:S(2)}, u32[]{:S(2)}) collective-permute-start(bf16[64,512]{1,0:T(8,128)(2,1)S(1)} %add_convert_fusion.2.refs_0_), channel_id=1, source_target_pairs={{0,3},{1,2},{2,1},{3,0},{4,7},{5,6},{6,5},{7,4},{8,11},{9,10},{10,... | collective-permute-start | bytes 196616 | tf_op jit(solution)/shard_map/ppermute | solution.py:480
  207.9 6.2 %collective-permute-start.14 = (bf16[64,512]{1,0:T(8,128)(2,1)S(1)}, bf16[64,512]{1,0:T(8,128)(2,1)S(1)}, u32[]{:S(2)}, u32[]{:S(2)}) collective-permute-start(bf16[64,512]{1,0:T(8,128)(2,1)S(1)} %add_convert_fusion.2.refs_0_), channel_id=1, source_target_pairs={{0,2},{1,3},{2,0},{3,1},{4,6},{5,7},{6,4},{7,5},{8,10},{9,11},{10,... | collective-permute-start | bytes 196616 | tf_op jit(solution)/shard_map/ppermute | solution.py:480
  208.7 5.5 %collective-permute-start.13 = (bf16[64,512]{1,0:T(8,128)(2,1)S(1)}, bf16[64,512]{1,0:T(8,128)(2,1)S(1)}, u32[]{:S(2)}, u32[]{:S(2)}) collective-permute-start(bf16[64,512]{1,0:T(8,128)(2,1)S(1)} %add_convert_fusion.2.refs_0_), channel_id=1, source_target_pairs={{0,1},{1,0},{2,3},{3,2},{4,5},{5,4},{6,7},{7,6},{8,9},{9,8},{10,11... | collective-permute-start | bytes 196616 | tf_op jit(solution)/shard_map/ppermute | solution.py:480
  214.1 1.3 collective-permute-start.24
  214.2 1.4 collective-permute-start.25
  214.7 1.3 collective-permute-start.26
  214.8 1.3 collective-permute-start.27
  (17 other events, 67.1 us)
where the time goes:
time: 218 us; the launch traced here: 217 us
  Pallas kernels  91 us (42%)
  waiting for transfers between devices  59 us (27%)
  starting transfers between devices  37.6 us (17%)
  local copies, waits for them, and re-layouts  21 us (10%)
  other arithmetic  7.16 us (3%)
    pallas_call x1, Pallas kernels, gate_matrices(): pl.pallas_call(kernel, grid_spec=pltpu.PrefetchScalarGridSpec(num_scalar_...  32 us
    all_to_all x2, waiting for transfers between devices, all_to_all(): return lax.all_to_all(value, 'dp', split_axis=0, concat_axis=0, tiled=True)  23.7 us
    ppermute x12, waiting for transfers between devices, over_blk(): return lax.ppermute(value, 'blk', [(i, i ^ step) for i in range(n_blk)])  21 us
    pallas_call x5, Pallas kernels, flip_cotangent(): pl.pallas_call(flip_kernel, grid=(last - first,), in_specs=[pl.BlockSpec(...  16.7 us
    ppermute x16, waiting for transfers between devices, over_dp(): return lax.ppermute(value, 'dp', [(i, i ^ step) for i in range(n_dp)])  14.4 us
    ppermute x12, starting transfers between devices, over_blk(): return lax.ppermute(value, 'blk', [(i, i ^ step) for i in range(n_blk)])  14.1 us
    pallas_call x2, Pallas kernels, update(): pl.pallas_call(functools.partial(update_kernel, degrees=degrees), in_spec...  13.5 us
    unnamed x39, local copies, waits for them, and re-layouts  12.6 us
  transfers between devices with their start and end apart: 30, of which 16 were waited for; matrix products, arithmetic and copies ran while one was open for 7% of the time, Pallas kernels for 38%

commit v1 on v0

--- a/solution.py
+++ b/solution.py
@@ -545,18 +545,15 @@
     own, other = z_halved(own)
     updated = update(gate, maps, local, width, MOST, total, None)
 
-    local = after(came_last, own, other, updated)
+    local = after(came_last, own, updated)
     near, far = outer_sum(place, gate, local, cots, width, LAST, pieces)
-    most = tree_sum([own, after(other, near)])
+    most = z_joined(tree_sum([own, after(other, near)]))
+    most = plane_gather(most, needed_degrees)
     last = plane_sum(chip_sum(near, far)).astype(jnp.bfloat16)
-    local = after(local, last)
-    others = [over_dp(last, 2 * step) for step in range(1, n_dp // 2)]
+    last = tree_sum([last] + [over_dp(last, 2 * step) for step in range(1, n_dp // 2)])
     updated = update(gate, maps, local, width, LAST, total, updated)
-    *others, updated = lax.optimization_barrier((*others, updated))
-    last = tree_sum([last, *others])
-    most = plane_gather(z_joined(most, *others), needed_degrees)
     mix_grad, out_grad = most_gradients(place, out_flipped, flipped, most, shard, piece)
-    last = plane_gather(after(last, updated), lambda own, at: own, mix_grad)
+    last = plane_gather(after(last, updated, *most), lambda own, at: own, mix_grad)
     mix_grad, out_grad = last_gradients(
         place, out_flipped, flipped, last, mix_grad, out_grad, piece
     )

time: 218 us -> 217 us (level)
  waiting for transfers between devices: 59 us -> 54.8 us
  other arithmetic: 7.16 us -> 9.58 us
    ppermute x12, waiting for transfers between devices: 21 us -> 12.4 us  [over_blk(): return lax.ppermute(value, 'blk', [(i, i ^ step) for i in range(n_blk)])]
    all_to_all x2, waiting for transfers between devices: 23.7 us -> 31.8 us  [all_to_all(): return lax.all_to_all(value, 'dp', split_axis=0, concat_axis=0, tiled=True)]
    ppermute x16, waiting for transfers between devices: 14.4 us -> 10.6 us  [over_dp(): return lax.ppermute(value, 'dp', [(i, i ^ step) for i in range(n_dp)])]
    ppermute x16, starting transfers between devices: 12.6 us -> 10.2 us  [over_dp(): return lax.ppermute(value, 'dp', [(i, i ^ step) for i in range(n_dp)])]
    unnamed x39 -> x37, local copies, waits for them, and re-layouts: 12.6 us -> 14.3 us
  transfers between devices with their start and end apart: 30 -> 30, of which waited for: 16 -> 16; matrix products, arithmetic and copies ran while one was open for 7% -> 8% of each run, Pallas kernels for 38% -> 40%
where the time goes in v1:
time: 217 us; the launch traced here: 215 us
  Pallas kernels  90.8 us (42%)
  waiting for transfers between devices  54.8 us (25%)
  starting transfers between devices  36.3 us (17%)
  local copies, waits for them, and re-layouts  22.7 us (10%)
  other arithmetic  9.58 us (4%)
    pallas_call x1, Pallas kernels, gate_matrices(): pl.pallas_call(kernel, grid_spec=pltpu.PrefetchScalarGridSpec(num_scalar_...  32 us
    all_to_all x2, waiting for transfers between devices, all_to_all(): return lax.all_to_all(value, 'dp', split_axis=0, concat_axis=0, tiled=True)  31.8 us
    pallas_call x5, Pallas kernels, flip_cotangent(): pl.pallas_call(flip_kernel, grid=(last - first,), in_specs=[pl.BlockSpec(...  16.7 us
    ppermute x12, starting transfers between devices, over_blk(): return lax.ppermute(value, 'blk', [(i, i ^ step) for i in range(n_blk)])  15.1 us
    unnamed x37, local copies, waits for them, and re-layouts  14.3 us
    pallas_call x2, Pallas kernels, update(): pl.pallas_call(functools.partial(update_kernel, degrees=degrees), in_spec...  13.3 us
    ppermute x12, waiting for transfers between devices, over_blk(): return lax.ppermute(value, 'blk', [(i, i ^ step) for i in range(n_blk)])  12.4 us
    pallas_call x2, Pallas kernels, outer_sum(): pl.pallas_call(functools.partial(outer_kernel, pieces=pieces, levels=leve...  11.5 us
  transfers between devices with their start and end apart: 30, of which 16 were waited for; matrix products, arithmetic and copies ran while one was open for 8% of the time, Pallas kernels for 40%

profile of v1, /device:TPU:0, one launch (start us, length us, event | category | flops | bytes accessed | tf_op | source)
XLA Modules:
  0.0 215.4 jit_solution(5088773522758663264)
XLA Ops:
  0.6 4.6 %pick_rows.2 = bf16[256,8192]{1,0:T(8,128)(2,1)} custom-call(s32[1,256]{1,0:T(1,128)} %order_ref.3, bf16[256,12800]{1,0:T(8,128)(2,1)} %rows_ref.2), custom_call_target="tpu_custom_call" | custom-call | tf_op jit(solution)/shard_map/pick_rows/pallas_call | solution.py:94
  5.3 6.3 %all-to-all-start = ((bf16[8,32,8192]{2,1,0:T(8,128)(2,1)}), bf16[8,32,8192]{2,1,0:T(8,128)(2,1)}, u32[]{:S(2)}, u32[]{:S(2)}) async-start(bf16[8,32,8192]{2,1,0:T(8,128)(2,1)} %bitcast.26), calls=%async_computation | async-start | bytes 8388608 | tf_op jit(solution)/shard_map/all_to_all | solution.py:483
  11.7 3.5 %pick_rows.3 = bf16[256,4608]{1,0:T(8,128)(2,1)} custom-call(s32[1,256]{1,0:T(1,128)} %order_ref.3, bf16[256,12800]{1,0:T(8,128)(2,1)} %rows_ref.2), custom_call_target="tpu_custom_call" | custom-call | tf_op jit(solution)/shard_map/pick_rows/pallas_call | solution.py:94
  15.2 32.0 %gate.1.gate_ref = bf16[5,256,256]{2,1,0:T(8,128)(2,1)S(1)} custom-call(s32[3,2]{1,0:T(4,128)S(1)} %copy.15.pairs_ref, s32[3,128,128]{2,1,0:T(8,128)S(1)} %copy-done.14, f32[3,128,128]{2,1,0:T(8,128)S(1)} %copy-done.15, bf16[16,512]{1,0:T(8,128)(2,1)S(1)} %fusion.7.weight_ref), custom_call_target="tpu_custom_call" | custom-call | flops 77309411328 | bytes 393216 | tf_op jit(solution)/shard_map/gate/pallas_call | solution.py:158
  48.3 2.2 %flip_cotangent.6.refs_1_ = bf16[512,768]{1,0:T(8,128)(2,1)S(1)} custom-call(bf16[256,12800]{1,0:T(8,128)(2,1)} %rows_ref.7), custom_call_target="tpu_custom_call" | custom-call | tf_op jit(solution)/shard_map/flip_cotangent/pallas_call | solution.py:205
  51.5 3.3 %flip_cotangent.7.refs_2_ = bf16[512,1280]{1,0:T(8,128)(2,1)S(1)} custom-call(bf16[256,12800]{1,0:T(8,128)(2,1)} %rows_ref.7), custom_call_target="tpu_custom_call" | custom-call | tf_op jit(solution)/shard_map/flip_cotangent/pallas_call | solution.py:205
  55.8 4.4 %flip_cotangent.8.refs_3_ = bf16[512,1792]{1,0:T(8,128)(2,1)S(1)} custom-call(bf16[256,12800]{1,0:T(8,128)(2,1)} %rows_ref.7), custom_call_target="tpu_custom_call" | custom-call | tf_op jit(solution)/shard_map/flip_cotangent/pallas_call | solution.py:205
  61.5 5.7 %flip_cotangent.9.refs_0_ = bf16[512,2304]{1,0:T(8,128)(2,1)S(1)} custom-call(bf16[256,12800]{1,0:T(8,128)(2,1)} %rows_ref.7), custom_call_target="tpu_custom_call" | custom-call | tf_op jit(solution)/shard_map/flip_cotangent/pallas_call | solution.py:205
  68.6 4.5 %degree_products.1.map_ref = bf16[2560,512]{1,0:T(8,128)(2,1)S(1)} custom-call(bf16[2560,512]{1,0:T(8,128)(2,1)S(1)} %copy-done.4, bf16[2560,512]{1,0:T(8,128)(2,1)} %right_ref), custom_call_target="tpu_custom_call" | custom-call | tf_op jit(solution)/shard_map/degree_products/pallas_call | solution.py:187
  74.6 3.0 %copy.16 = bf16[5,512,512]{1,2,0:T(8,128)(2,1)S(1)} copy(bf16[5,512,512]{2,1,0:T(8,128)(2,1)} %bitcast.25) | data formatting | bytes 5242880 | tf_op jit(solution)/shard_map/reshape | solution.py:537
  77.6 4.4 %copy.17 = bf16[5,512,512]{1,2,0:T(8,128)(2,1)} copy(bf16[5,512,512]{2,1,0:T(8,128)(2,1)} %bitcast.27) | data formatting | bytes 5242880 | tf_op jit(solution)/shard_map/reshape | solution.py:537
  82.0 23.7 %all-to-all-done = bf16[8,32,8192]{2,1,0:T(8,128)(2,1)} async-done(((bf16[8,32,8192]{2,1,0:T(8,128)(2,1)}), bf16[8,32,8192]{2,1,0:T(8,128)(2,1)}, u32[]{:S(2)}, u32[]{:S(2)}) %all-to-all-start) | async-done | bytes 4194336 | tf_op jit(solution)/shard_map/all_to_all | solution.py:483
  105.7 4.6 %all-to-all-start.1 = ((bf16[8,32,4608]{2,1,0:T(8,128)(2,1)}), bf16[8,32,4608]{2,1,0:T(8,128)(2,1)}, u32[]{:S(2)}, u32[]{:S(2)}) async-start(bf16[8,32,4608]{2,1,0:T(8,128)(2,1)} %bitcast.28), calls=%async_computation.1 | async-start | bytes 4718592 | tf_op jit(solution)/shard_map/all_to_all | solution.py:483
  114.3 7.6 %outer_sum.2 = (f32[1024,512]{1,0:T(8,128)}, bf16[1024,512]{1,0:T(8,128)(2,1)S(1)}) custom-call(s32[3]{0:T(128)S(1)} %pad_add_fusion.place_ref, bf16[5,256,256]{2,1,0:T(8,128)(2,1)S(1)} %gate.1.gate_ref, bf16[256,8192]{1,0:T(8,128)(2,1)} %bitcast.2.local_ref, bf16[512,256]{1,0:T(8,128)(2,1)S(1)} %flip_cotangent.5.refs_0_, bf16[512,768]{1,0:T(8,128)(2,1)S(1)} %copy-done.12, ...), custom_call_target="tpu_custom_call" | custom-call | flops 3221225472 | bytes 8388608 | tf_op jit(solution)/shard_map/outer_sum/pallas_call | solution.py:250
  122.1 2.5 %collective-permute-done = bf16[1024,512]{1,0:T(8,128)(2,1)S(1)} collective-permute-done((bf16[1024,512]{1,0:T(8,128)(2,1)S(1)}, bf16[1024,512]{1,0:T(8,128)(2,1)S(1)}, u32[]{:S(2)}, u32[]{:S(2)}) %collective-permute-start) | collective-permute-done | bytes 1048608 | tf_op jit(solution)/shard_map/ppermute | solution.py:477
  124.6 3.3 %fusion.10 = (bf16[1024,512]{1,0:T(8,128)(2,1)S(1)}, f32[1024,512]{1,0:T(8,128)}) fusion(f32[1024,512]{1,0:T(8,128)} %get-tuple-element.32, bf16[1024,512]{1,0:T(8,128)(2,1)S(1)} %collective-permute-done), kind=kLoop, calls=%fused_computation.28 | loop fusion | flops 1572864 | bytes 6291456 | tf_op jit(solution)/shard_map/convert.5
  128.8 2.5 %collective-permute-start.3 = (bf16[256,512]{1,0:T(8,128)(2,1)}, bf16[256,512]{1,0:T(8,128)(2,1)S(1)}, u32[]{:S(2)}, u32[]{:S(2)}) collective-permute-start(bf16[256,512]{1,0:T(8,128)(2,1)} %get-tuple-element.54), channel_id=1, source_target_pairs={{0,3},{1,2},{2,1},{3,0},{4,7},{5,6},{6,5},{7,4},{8,11},{9,10},{10,... | collective-permute-start | bytes 786440 | tf_op jit(solution)/shard_map/ppermute | solution.py:480
  132.3 6.8 %collective-permute-done.3 = bf16[256,512]{1,0:T(8,128)(2,1)S(1)} collective-permute-done((bf16[256,512]{1,0:T(8,128)(2,1)}, bf16[256,512]{1,0:T(8,128)(2,1)S(1)}, u32[]{:S(2)}, u32[]{:S(2)}) %collective-permute-start.3) | collective-permute-done | bytes 262176 | tf_op jit(solution)/shard_map/ppermute | solution.py:480
  139.1 4.9 %collective-permute-done.2 = bf16[256,512]{1,0:T(8,128)(2,1)} collective-permute-done((bf16[256,512]{1,0:T(8,128)(2,1)}, bf16[256,512]{1,0:T(8,128)(2,1)}, u32[]{:S(2)}, u32[]{:S(2)}) %collective-permute-start.2) | collective-permute-done | bytes 262176 | tf_op jit(solution)/shard_map/ppermute | solution.py:480
  145.5 1.7 collective-permute-start.4
  147.2 1.7 copy-done.2
  149.0 7.9 %update.2.refs_0_ = bf16[256,12800]{1,0:T(8,128)(2,1)} custom-call(bf16[5,256,256]{2,1,0:T(8,128)(2,1)S(1)} %gate.1.gate_ref, bf16[2560,512]{1,0:T(8,128)(2,1)S(1)} %copy-done.2, bf16[256,8192]{1,0:T(8,128)(2,1)} %bitcast.2.local_ref), custom_call_target="tpu_custom_call" | custom-call | flops 3221225472 | bytes 8388608 | tf_op jit(solution)/shard_map/update/pallas_call | solution.py:306
  157.6 2.4 %collective-permute-start.12 = (bf16[128,512]{1,0:T(8,128)(2,1)}, bf16[128,512]{1,0:T(8,128)(2,1)}, u32[]{:S(2)}, u32[]{:S(2)}) collective-permute-start(bf16[128,512]{1,0:T(8,128)(2,1)} %add_convert_fusion.1), channel_id=1, source_target_pairs={{0,16},{4,20},{8,24},{12,28},{16,0},{20,4},{24,8},{28,12},{1,17},{... | collective-permute-start | bytes 393224 | tf_op jit(solution)/shard_map/ppermute | solution.py:477
  160.0 8.1 %all-to-all-done.1 = bf16[8,32,4608]{2,1,0:T(8,128)(2,1)} async-done(((bf16[8,32,4608]{2,1,0:T(8,128)(2,1)}), bf16[8,32,4608]{2,1,0:T(8,128)(2,1)}, u32[]{:S(2)}, u32[]{:S(2)}) %all-to-all-start.1) | async-done | bytes 2359328 | tf_op jit(solution)/shard_map/all_to_all | solution.py:483
  168.1 1.7 copy-done.6
  169.7 4.0 %outer_sum.3 = (f32[256,512]{1,0:T(8,128)S(1)}, bf16[256,512]{1,0:T(8,128)(2,1)S(1)}) custom-call(s32[3]{0:T(128)S(1)} %pad_add_fusion.place_ref, bf16[5,256,256]{2,1,0:T(8,128)(2,1)S(1)} %gate.1.gate_ref, bf16[256,4608]{1,0:T(8,128)(2,1)} %bitcast.10.local_ref, bf16[512,2304]{1,0:T(8,128)(2,1)S(1)} %copy-done.6), custom_call_target="tpu_custom_call" | custom-call | flops 1811939328 | bytes 4718592 | tf_op jit(solution)/shard_map/outer_sum/pallas_call | solution.py:250
  174.5 1.7 add_convert_fusion
  176.2 6.2 %collective-permute-done.13 = bf16[128,512]{1,0:T(8,128)(2,1)} collective-permute-done((bf16[128,512]{1,0:T(8,128)(2,1)}, bf16[128,512]{1,0:T(8,128)(2,1)}, u32[]{:S(2)}, u32[]{:S(2)}) %collective-permute-start.13) | collective-permute-done | bytes 131104 | tf_op jit(solution)/shard_map/ppermute | solution.py:477
  184.8 2.5 %collective-permute-start.8 = (bf16[64,512]{1,0:T(8,128)(2,1)S(1)}, bf16[64,512]{1,0:T(8,128)(2,1)S(1)}, u32[]{:S(2)}, u32[]{:S(2)}) collective-permute-start(bf16[64,512]{1,0:T(8,128)(2,1)S(1)} %get-tuple-element.61), channel_id=1, source_target_pairs={{0,3},{1,2},{2,1},{3,0},{4,7},{5,6},{6,5},{7,4},{8,11},{9,10},{10,... | collective-permute-start | bytes 196616 | tf_op jit(solution)/shard_map/ppermute | solution.py:480
  195.7 1.9 collective-permute-start.9
  197.5 5.4 %update.3 = bf16[256,12800]{1,0:T(8,128)(2,1)} custom-call(bf16[5,256,256]{2,1,0:T(8,128)(2,1)S(1)} %gate.1.gate_ref, bf16[2560,512]{1,0:T(8,128)(2,1)S(1)} %copy-done.3, bf16[256,4608]{1,0:T(8,128)(2,1)} %bitcast.10.local_ref, bf16[256,12800]{1,0:T(8,128)(2,1)} %update.2.refs_0_), custom_call_target="tpu_custom_call", output_to_operand_aliasing={{}: (3, {})} | custom-call | flops 1811939328 | bytes 4718592 | tf_op jit(solution)/shard_map/update/pallas_call | solution.py:306
  208.6 3.9 %most_gradients.1 = (f32[640,512]{1,0:T(8,128)}, f32[640,512]{1,0:T(8,128)}) custom-call(s32[3]{0:T(128)S(1)} %pad_add_fusion.place_ref, bf16[2560,512]{1,0:T(8,128)(2,1)S(1)} %bitcast.23, bf16[2560,512]{1,0:T(8,128)(2,1)S(1)} %bitcast.21, bf16[128,512]{1,0:T(8,128)(2,1)S(1)} %get-tuple-element.59.refs_0_, ...), custom_call_target="tpu_custom_call" | custom-call | tf_op jit(solution)/shard_map/most_gradients/pallas_call | solution.py:366
  (97 shorter events, 35.3 us)
Async XLA Ops:
  5.3 100.5 %all-to-all-start = ((bf16[8,32,8192]{2,1,0:T(8,128)(2,1)}), bf16[8,32,8192]{2,1,0:T(8,128)(2,1)}, u32[]{:S(2)}, u32[]{:S(2)}) async-start(bf16[8,32,8192]{2,1,0:T(8,128)(2,1)} %bitcast.26), calls=%async_computation | async-start | bytes 8388608 | tf_op jit(solution)/shard_map/all_to_all | solution.py:483
  105.7 62.4 %all-to-all-start.1 = ((bf16[8,32,4608]{2,1,0:T(8,128)(2,1)}), bf16[8,32,4608]{2,1,0:T(8,128)(2,1)}, u32[]{:S(2)}, u32[]{:S(2)}) async-start(bf16[8,32,4608]{2,1,0:T(8,128)(2,1)} %bitcast.28), calls=%async_computation.1 | async-start | bytes 4718592 | tf_op jit(solution)/shard_map/all_to_all | solution.py:483
  121.9 2.7 %collective-permute-start = (bf16[1024,512]{1,0:T(8,128)(2,1)S(1)}, bf16[1024,512]{1,0:T(8,128)(2,1)S(1)}, u32[]{:S(2)}, u32[]{:S(2)}) collective-permute-start(bf16[1024,512]{1,0:T(8,128)(2,1)S(1)} %get-tuple-element.33), channel_id=1, source_target_pairs={{0,4},{4,0},{8,12},{12,8},{16,20},{20,16},{24,28},{28,24},{1,5},{5... | collective-permute-start | bytes 3145736 | tf_op jit(solution)/shard_map/ppermute | solution.py:477
  128.8 10.3 %collective-permute-start.3 = (bf16[256,512]{1,0:T(8,128)(2,1)}, bf16[256,512]{1,0:T(8,128)(2,1)S(1)}, u32[]{:S(2)}, u32[]{:S(2)}) collective-permute-start(bf16[256,512]{1,0:T(8,128)(2,1)} %get-tuple-element.54), channel_id=1, source_target_pairs={{0,3},{1,2},{2,1},{3,0},{4,7},{5,6},{6,5},{7,4},{8,11},{9,10},{10,... | collective-permute-start | bytes 786440 | tf_op jit(solution)/shard_map/ppermute | solution.py:480
  131.3 12.8 %collective-permute-start.2 = (bf16[256,512]{1,0:T(8,128)(2,1)}, bf16[256,512]{1,0:T(8,128)(2,1)}, u32[]{:S(2)}, u32[]{:S(2)}) collective-permute-start(bf16[256,512]{1,0:T(8,128)(2,1)} %get-tuple-element.55), channel_id=1, source_target_pairs={{0,2},{1,3},{2,0},{3,1},{4,6},{5,7},{6,4},{7,5},{8,10},{9,11},{10,... | collective-permute-start | bytes 786440 | tf_op jit(solution)/shard_map/ppermute | solution.py:480
  131.8 12.3 %collective-permute-start.1 = (bf16[256,512]{1,0:T(8,128)(2,1)}, bf16[256,512]{1,0:T(8,128)(2,1)}, u32[]{:S(2)}, u32[]{:S(2)}) collective-permute-start(bf16[256,512]{1,0:T(8,128)(2,1)} %get-tuple-element.53), channel_id=1, source_target_pairs={{0,1},{1,0},{2,3},{3,2},{4,5},{5,4},{6,7},{7,6},{8,9},{9,8},{10,11... | collective-permute-start | bytes 786440 | tf_op jit(solution)/shard_map/ppermute | solution.py:480
  145.5 11.3 %collective-permute-start.4 = (bf16[128,512]{1,0:T(8,128)(2,1)S(1)}, bf16[128,512]{1,0:T(8,128)(2,1)S(1)}, u32[]{:S(2)}, u32[]{:S(2)}) collective-permute-start(bf16[128,512]{1,0:T(8,128)(2,1)S(1)} %select_convert_fusion), channel_id=1, source_target_pairs={{0,8},{4,12},{8,0},{12,4},{16,24},{20,28},{24,16},{28,20},{1,9},{5... | collective-permute-start | bytes 393224 | tf_op jit(solution)/shard_map/ppermute | solution.py:477
  157.6 16.9 %collective-permute-start.12 = (bf16[128,512]{1,0:T(8,128)(2,1)}, bf16[128,512]{1,0:T(8,128)(2,1)}, u32[]{:S(2)}, u32[]{:S(2)}) collective-permute-start(bf16[128,512]{1,0:T(8,128)(2,1)} %add_convert_fusion.1), channel_id=1, source_target_pairs={{0,16},{4,20},{8,24},{12,28},{16,0},{20,4},{24,8},{28,12},{1,17},{... | collective-permute-start | bytes 393224 | tf_op jit(solution)/shard_map/ppermute | solution.py:477
  174.5 9.1 %collective-permute-start.5 = (bf16[256,512]{1,0:T(8,128)(2,1)S(1)}, bf16[256,512]{1,0:T(8,128)(2,1)}, u32[]{:S(2)}, u32[]{:S(2)}) collective-permute-start(bf16[256,512]{1,0:T(8,128)(2,1)S(1)} %get-tuple-element.36), channel_id=1, source_target_pairs={{0,4},{4,0},{8,12},{12,8},{16,20},{20,16},{24,28},{28,24},{1,5},{5... | collective-permute-start | bytes 786440 | tf_op jit(solution)/shard_map/ppermute | solution.py:477
  176.2 6.2 %collective-permute-start.13 = (bf16[128,512]{1,0:T(8,128)(2,1)}, bf16[128,512]{1,0:T(8,128)(2,1)}, u32[]{:S(2)}, u32[]{:S(2)}) collective-permute-start(bf16[128,512]{1,0:T(8,128)(2,1)} %add_convert_fusion), channel_id=1, source_target_pairs={{0,8},{4,12},{8,0},{12,4},{16,24},{20,28},{24,16},{28,20},{1,9},{5... | collective-permute-start | bytes 393224 | tf_op jit(solution)/shard_map/ppermute | solution.py:477
  176.2 21.4 %copy-start.3 = (bf16[2560,512]{1,0:T(8,128)(2,1)S(1)}, bf16[2560,512]{1,0:T(8,128)(2,1)}, u32[]{:S(2)}) copy-start(bf16[2560,512]{1,0:T(8,128)(2,1)} %copy-done.1) | copy-start | bytes 7864324
  184.8 6.7 %collective-permute-start.8 = (bf16[64,512]{1,0:T(8,128)(2,1)S(1)}, bf16[64,512]{1,0:T(8,128)(2,1)S(1)}, u32[]{:S(2)}, u32[]{:S(2)}) collective-permute-start(bf16[64,512]{1,0:T(8,128)(2,1)S(1)} %get-tuple-element.61), channel_id=1, source_target_pairs={{0,3},{1,2},{2,1},{3,0},{4,7},{5,6},{6,5},{7,4},{8,11},{9,10},{10,... | collective-permute-start | bytes 196616 | tf_op jit(solution)/shard_map/ppermute | solution.py:480
  187.3 5.7 %collective-permute-start.7 = (bf16[64,512]{1,0:T(8,128)(2,1)S(1)}, bf16[64,512]{1,0:T(8,128)(2,1)S(1)}, u32[]{:S(2)}, u32[]{:S(2)}) collective-permute-start(bf16[64,512]{1,0:T(8,128)(2,1)S(1)} %get-tuple-element.62), channel_id=1, source_target_pairs={{0,2},{1,3},{2,0},{3,1},{4,6},{5,7},{6,4},{7,5},{8,10},{9,11},{10,... | collective-permute-start | bytes 196616 | tf_op jit(solution)/shard_map/ppermute | solution.py:480
  187.8 5.2 %collective-permute-start.6 = (bf16[64,512]{1,0:T(8,128)(2,1)S(1)}, bf16[64,512]{1,0:T(8,128)(2,1)S(1)}, u32[]{:S(2)}, u32[]{:S(2)}) collective-permute-start(bf16[64,512]{1,0:T(8,128)(2,1)S(1)} %get-tuple-element.60), channel_id=1, source_target_pairs={{0,1},{1,0},{2,3},{3,2},{4,5},{5,4},{6,7},{7,6},{8,9},{9,8},{10,11... | collective-permute-start | bytes 196616 | tf_op jit(solution)/shard_map/ppermute | solution.py:480
  188.4 7.3 %collective-permute-start.14 = (bf16[128,512]{1,0:T(8,128)(2,1)S(1)}, bf16[128,512]{1,0:T(8,128)(2,1)S(1)}, u32[]{:S(2)}, u32[]{:S(2)}) collective-permute-start(bf16[128,512]{1,0:T(8,128)(2,1)S(1)} %get-tuple-element.58), channel_id=1, source_target_pairs={{0,1},{1,0},{2,3},{3,2},{4,5},{5,4},{6,7},{7,6},{8,9},{9,8},{10,11... | collective-permute-start | bytes 393224 | tf_op jit(solution)/shard_map/ppermute | solution.py:480
  189.9 13.0 %collective-permute-start.15 = (bf16[128,512]{1,0:T(8,128)(2,1)S(1)}, bf16[128,512]{1,0:T(8,128)(2,1)S(1)}, u32[]{:S(2)}, u32[]{:S(2)}) collective-permute-start(bf16[128,512]{1,0:T(8,128)(2,1)S(1)} %get-tuple-element.57), channel_id=1, source_target_pairs={{0,2},{1,3},{2,0},{3,1},{4,6},{5,7},{6,4},{7,5},{8,10},{9,11},{10,... | collective-permute-start | bytes 393224 | tf_op jit(solution)/shard_map/ppermute | solution.py:480
  191.5 11.6 %collective-permute-start.16 = (bf16[128,512]{1,0:T(8,128)(2,1)S(1)}, bf16[128,512]{1,0:T(8,128)(2,1)S(1)}, u32[]{:S(2)}, u32[]{:S(2)}) collective-permute-start(bf16[128,512]{1,0:T(8,128)(2,1)S(1)} %get-tuple-element.56), channel_id=1, source_target_pairs={{0,3},{1,2},{2,1},{3,0},{4,7},{5,6},{6,5},{7,4},{8,11},{9,10},{10,... | collective-permute-start | bytes 393224 | tf_op jit(solution)/shard_map/ppermute | solution.py:480
  193.1 15.5 %copy-start = (bf16[5,512,512]{1,2,0:T(8,128)(2,1)S(1)}, bf16[5,512,512]{1,2,0:T(8,128)(2,1)}, u32[]{:S(2)}) copy-start(bf16[5,512,512]{1,2,0:T(8,128)(2,1)} %copy.17) | copy-start | bytes 7864324
  193.1 10.5 %collective-permute-start.11 = (bf16[64,512]{1,0:T(8,128)(2,1)S(1)}, bf16[64,512]{1,0:T(8,128)(2,1)S(1)}, u32[]{:S(2)}, u32[]{:S(2)}) collective-permute-start(bf16[64,512]{1,0:T(8,128)(2,1)S(1)} %fusion.4), channel_id=1, source_target_pairs={{0,24},{4,28},{8,16},{12,20},{16,8},{20,12},{24,0},{28,4},{1,25},{... | collective-permute-start | bytes 196616 | tf_op jit(solution)/shard_map/ppermute | solution.py:477
  193.9 9.7 %collective-permute-start.10 = (bf16[64,512]{1,0:T(8,128)(2,1)S(1)}, bf16[64,512]{1,0:T(8,128)(2,1)S(1)}, u32[]{:S(2)}, u32[]{:S(2)}) collective-permute-start(bf16[64,512]{1,0:T(8,128)(2,1)S(1)} %fusion.4), channel_id=1, source_target_pairs={{0,16},{4,20},{8,24},{12,28},{16,0},{20,4},{24,8},{28,12},{1,17},{... | collective-permute-start | bytes 196616 | tf_op jit(solution)/shard_map/ppermute | solution.py:477
  195.7 8.4 %collective-permute-start.9 = (bf16[64,512]{1,0:T(8,128)(2,1)S(1)}, bf16[64,512]{1,0:T(8,128)(2,1)S(1)}, u32[]{:S(2)}, u32[]{:S(2)}) collective-permute-start(bf16[64,512]{1,0:T(8,128)(2,1)S(1)} %fusion.4), channel_id=1, source_target_pairs={{0,8},{4,12},{8,0},{12,4},{16,24},{20,28},{24,16},{28,20},{1,9},{5... | collective-permute-start | bytes 196616 | tf_op jit(solution)/shard_map/ppermute | solution.py:477
  203.0 1.4 collective-permute-start.17
  203.1 1.5 collective-permute-start.18
  203.6 1.3 collective-permute-start.19
  203.6 1.4 collective-permute-start.20
  205.1 7.4 %collective-permute-start.21 = (bf16[64,512]{1,0:T(8,128)(2,1)S(1)}, bf16[64,512]{1,0:T(8,128)(2,1)S(1)}, u32[]{:S(2)}, u32[]{:S(2)}) collective-permute-start(bf16[64,512]{1,0:T(8,128)(2,1)S(1)} %add_convert_fusion.2.refs_0_), channel_id=1, source_target_pairs={{0,1},{1,0},{2,3},{3,2},{4,5},{5,4},{6,7},{7,6},{8,9},{9,8},{10,11... | collective-permute-start | bytes 196616 | tf_op jit(solution)/shard_map/ppermute | solution.py:480
  205.6 7.5 %collective-permute-start.22 = (bf16[64,512]{1,0:T(8,128)(2,1)S(1)}, bf16[64,512]{1,0:T(8,128)(2,1)S(1)}, u32[]{:S(2)}, u32[]{:S(2)}) collective-permute-start(bf16[64,512]{1,0:T(8,128)(2,1)S(1)} %add_convert_fusion.2.refs_0_), channel_id=1, source_target_pairs={{0,2},{1,3},{2,0},{3,1},{4,6},{5,7},{6,4},{7,5},{8,10},{9,11},{10,... | collective-permute-start | bytes 196616 | tf_op jit(solution)/shard_map/ppermute | solution.py:480
  207.0 6.1 %collective-permute-start.23 = (bf16[64,512]{1,0:T(8,128)(2,1)S(1)}, bf16[64,512]{1,0:T(8,128)(2,1)S(1)}, u32[]{:S(2)}, u32[]{:S(2)}) collective-permute-start(bf16[64,512]{1,0:T(8,128)(2,1)S(1)} %add_convert_fusion.2.refs_0_), channel_id=1, source_target_pairs={{0,3},{1,2},{2,1},{3,0},{4,7},{5,6},{6,5},{7,4},{8,11},{9,10},{10,... | collective-permute-start | bytes 196616 | tf_op jit(solution)/shard_map/ppermute | solution.py:480
  212.5 1.3 collective-permute-start.24
  212.5 1.4 collective-permute-start.25
  213.1 1.3 collective-permute-start.26
  213.1 1.3 collective-permute-start.27
  (16 other events, 38.2 us)
